TPU v7x, 512 devices: a whole 4x4x16 slice. The times are simulated.
512 devices in a mesh: rows: 8 (over x, core), cols: 8 (over z_lo), depth: 8 (over z_hi, y).
Axes of the slice: x: 4, y: 4, z: 16 (z_hi: 2, z_lo: 8; z = z_hi * 8 + z_lo), core: 2. Of those that a mesh axis runs over, the one named last changes fastest.
Arguments:
- activations: bfloat16 [512, 8192], P(('cols', 'depth'), 'rows'), may hold values from -6 to 6
- out_grad: bfloat16 [512, 8192], P(('cols', 'depth'), 'rows'), may hold values from -1.5 to 1.5
- w_gate: bfloat16 [8192, 16384], P('rows', ('cols', 'depth')), may hold values from -0.0625 to 0.0625
- w_up: bfloat16 [8192, 16384], P('rows', ('cols', 'depth')), may hold values from -0.0625 to 0.0625
- w_down: bfloat16 [16384, 8192], P(('cols', 'depth'), 'rows'), may hold values from -0.046875 to 0.046875
Outputs:
- input_grad: bfloat16 [512, 8192], P(('cols', 'depth'), 'rows')
- gate_grad: bfloat16 [8192, 16384], P('rows', ('cols', 'depth'))
- up_grad: bfloat16 [8192, 16384], P('rows', ('cols', 'depth'))
- down_grad: bfloat16 [16384, 8192], P(('cols', 'depth'), 'rows')
All inputs are finite; a program needn't handle non-finite values.
Results may differ from a plain program's by a relative error of at most 0.0049.
Values may be sent and summed in bfloat16 or wider, within the bound.
A program may use at most 64 MiB of HBM per device.

v0:
```python
import jax
import jax.numpy as jnp
from jax import lax
from jax.sharding import PartitionSpec as P


def pointwise(gate, up, hid_grad):
    sigm = jax.nn.sigmoid(gate)
    hidden = (gate * sigm * up).astype(jnp.bfloat16)
    gate_delta = (hid_grad * up * sigm * (1.0 + gate * (1.0 - sigm))).astype(jnp.bfloat16)
    up_delta = (hid_grad * gate * sigm).astype(jnp.bfloat16)
    return (hidden, gate_delta, up_delta)


def body(activations, out_grad, w_gate, w_up, w_down):
    acts_all, grads_all = (
        lax.all_gather(activations, ("cols", "depth"), axis=0, tiled=True),
        lax.all_gather(out_grad, ("cols", "depth"), axis=0, tiled=True),
    )
    gate_part = jnp.dot(acts_all, w_gate, preferred_element_type=jnp.float32)
    up_part = jnp.dot(acts_all, w_up, preferred_element_type=jnp.float32)
    hid_part = jnp.einsum("td,fd->tf", grads_all, w_down, preferred_element_type=jnp.float32)
    gate, up, hid_grad = lax.psum((gate_part, up_part, hid_part), "rows")
    hidden, gate_delta, up_delta = pointwise(gate, up, hid_grad)
    down_grad = jnp.einsum(
        "tf,td->fd", hidden, grads_all, preferred_element_type=jnp.float32
    ).astype(jnp.bfloat16)
    gate_grad = jnp.einsum(
        "td,tf->df", acts_all, gate_delta, preferred_element_type=jnp.float32
    ).astype(jnp.bfloat16)
    up_grad = jnp.einsum(
        "td,tf->df", acts_all, up_delta, preferred_element_type=jnp.float32
    ).astype(jnp.bfloat16)
    input_term = jnp.einsum("tf,df->td", gate_delta, w_gate, preferred_element_type=jnp.float32)
    input_term = input_term + jnp.einsum(
        "tf,df->td", up_delta, w_up, preferred_element_type=jnp.float32
    )
    input_grad = lax.psum_scatter(
        input_term, ("cols", "depth"), scatter_dimension=0, tiled=True
    ).astype(jnp.bfloat16)
    return (input_grad, gate_grad, up_grad, down_grad)


def solution(mesh):
    in_specs = (
        P(("cols", "depth"), "rows"),
        P(("cols", "depth"), "rows"),
        P("rows", ("cols", "depth")),
        P("rows", ("cols", "depth")),
        P(("cols", "depth"), "rows"),
    )
    out_specs = (
        P(("cols", "depth"), "rows"),
        P("rows", ("cols", "depth")),
        P("rows", ("cols", "depth")),
        P(("cols", "depth"), "rows"),
    )
    return jax.shard_map(body, mesh=mesh, in_specs=in_specs, out_specs=out_specs, check_vma=False)
```

profile of v0, /device:TPU:24, one launch (start us, length us, event | category | flops | bytes accessed | tf_op | source)
XLA Modules:
  0.0 1614.6 jit_solution(2915994375072521250)
XLA Ops:
  7.2 0.0 copy-start
  7.2 0.0 copy-start.2
  7.2 0.0 all-gather.5.cloned.1.call-start
  7.2 0.7 all-gather.5.cloned.1.call-update
  7.9 0.0 all-gather.3.cloned.1.call-start
  8.0 0.7 all-gather.3.cloned.1.call-update
  8.7 0.0 copy-start.4
  8.7 0.0 all-reduce.3.cloned.1.call-start
  8.7 491.0 %all-gather.5.cloned.1.call-done = bf16[512,1024]{1,0:T(8,128)(2,1)} async-done(((bf16[8,1024]{1,0:T(8,128)(2,1)}), bf16[512,1024]{1,0:T(8,128)(2,1)}) %all-gather.5.cloned.1.call-update) | async-done | bytes 1048592 | tf_op jit(solution)/shard_map/all_gather | solution.py:17
  499.8 0.0 copy-done
  499.8 0.0 copy-start.1
  499.8 2.5 fusion.6
  502.3 0.0 copy-done.2
  502.3 0.0 copy-done.1
  502.3 1.2 fusion.5
  503.5 483.1 %all-gather.3.cloned.1.call-done = bf16[512,1024]{1,0:T(8,128)(2,1)} async-done(((bf16[8,1024]{1,0:T(8,128)(2,1)}), bf16[512,1024]{1,0:T(8,128)(2,1)}) %all-gather.3.cloned.1.call-update) | async-done | bytes 1048592 | tf_op jit(solution)/shard_map/all_gather | solution.py:18
  986.6 0.0 copy-done.4
  986.6 2.5 fusion.4
  989.1 0.0 all-reduce.3.cloned.1.call-update
  989.1 0.0 reduce-scatter.2.cloned.1.call-start
  989.2 79.5 %all-reduce.3.cloned.1.call-done = (f32[512,256]{1,0:T(8,128)}, f32[512,256]{1,0:T(8,128)}, f32[512,256]{1,0:T(8,128)}) async-done(((f32[512,256]{1,0:T(8,128)}, f32[512,256]{1,0:T(8,128)}, f32[512,256]{1,0:T(8,128)}), (f32[512,256]{1,0:T(8,128)}, f32[512,256]{1,0:T(8,128)}, f32[512,256]{1,0:T(8,128)})) %all-reduce.3.cloned.1.call-update) | async-done | bytes 1572880 | tf_op jit(solution)/shard_map/psum | solution.py:23
  1068.7 1.6 multiply_convert_fusion.1
  1070.3 0.5 fusion.7
  1070.8 1.8 convolution_add_fusion
  1072.6 0.0 reduce-scatter.2.cloned.1.call-update
  1072.6 0.5 fusion
  1073.1 0.0 copy-start.3
  1073.1 1.0 copy.9
  1074.1 0.5 fusion.1
  1074.5 1.0 copy.10
  1075.5 0.0 copy-done.3
  1075.5 2.5 convolution_convert_fusion
  1078.0 528.7 %reduce-scatter.2.cloned.1.call-done = f32[8,1024]{1,0:T(8,128)} async-done(((f32[512,1024]{1,0:T(8,128)}), f32[8,1024]{1,0:T(8,128)}) %reduce-scatter.2.cloned.1.call-update) | async-done | bytes 32784 | tf_op jit(solution)/shard_map/reduce_scatter | solution.py:38
  1606.7 1.4 convert_element_type.29
Async XLA Ops:
  7.2 492.6 %copy-start = (bf16[1024,256]{1,0:T(8,128)(2,1)S(1)}, bf16[1024,256]{1,0:T(8,128)(2,1)}, u32[]{:S(2)}) copy-start(bf16[1024,256]{1,0:T(8,128)(2,1)} %param.7) | copy-start | bytes 1572868
  7.2 495.1 %copy-start.2 = (bf16[1024,256]{1,0:T(8,128)(2,1)S(1)}, bf16[1024,256]{1,0:T(8,128)(2,1)}, u32[]{:S(2)}) copy-start(bf16[1024,256]{1,0:T(8,128)(2,1)} %param.8) | copy-start | bytes 1572868
  7.2 492.6 %all-gather.5.cloned.1.call-start = ((), (), s32[]{:S(2)}) async-start(), calls=%async_computation.2 | async-start | bytes 1064960 | tf_op jit(solution)/shard_map/all_gather | solution.py:17
  7.9 978.7 %all-gather.3.cloned.1.call-start = ((), (), s32[]{:S(2)}) async-start(), calls=%async_computation.1 | async-start | bytes 1064960 | tf_op jit(solution)/shard_map/all_gather | solution.py:18
  8.7 977.9 %copy-start.4 = (bf16[256,1024]{1,0:T(8,128)(2,1)S(1)}, bf16[256,1024]{1,0:T(8,128)(2,1)}, u32[]{:S(2)}) copy-start(bf16[256,1024]{1,0:T(8,128)(2,1)} %param.9) | copy-start | bytes 1572868
  8.7 1060.0 %all-reduce.3.cloned.1.call-start = ((), (), s32[]{:S(2)}) async-start(), calls=%async_computation.4 | async-start | bytes 3145728 | tf_op jit(solution)/shard_map/psum | solution.py:23
  499.8 2.6 copy-start.1
  989.1 617.6 %reduce-scatter.2.cloned.1.call-start = ((), (), s32[]{:S(2)}) async-start(), calls=%async_computation.3 | async-start | bytes 2129920 | tf_op jit(solution)/shard_map/reduce_scatter | solution.py:38
  1073.1 2.5 copy-start.3
Sparse Core Ops, SparseCore 0:
  10.1 489.6 all-gather.4
  501.8 484.7 all-gather.2
  989.8 78.8 all-reduce.2
  1072.7 533.9 reduce-scatter.1
where the time goes:
time: 1610 us
  waiting for transfers between devices  1580 us (98%)
    reduce_scatter x1, waiting for transfers between devices, body(): lax.psum_scatter(input_term, ('cols', 'depth'), scatter_dimension=0, tile...  529 us
    all_gather x1, waiting for transfers between devices, body(): lax.all_gather(activations, ('cols', 'depth'), axis=0, tiled=True)  491 us
    all_gather x1, waiting for transfers between devices, body(): lax.all_gather(out_grad, ('cols', 'depth'), axis=0, tiled=True)  483 us
    psum x1, waiting for transfers between devices, body(): gate, up, hid_grad = lax.psum((gate_part, up_part, hid_part), 'rows')  79.5 us
  transfers between devices with their start and end apart: 4, of which 4 were waited for; matrix products, arithmetic and copies ran while one was open for 1% of the time, Pallas kernels for 0%

commit v1 on v0

v1 whole, which is shorter than its diff:
```python
import jax
import jax.numpy as jnp
from jax import lax
from jax.experimental import pallas as pl
from jax.experimental.pallas import tpu as pltpu
from jax.sharding import PartitionSpec as P

BF = jnp.bfloat16
F32 = jnp.float32
NR, NY, NZ, ZLO = 8, 4, 16, 8
CHUNKS = 4
NT = (((1,), (1,)), ((), ()))
TN = (((0,), (0,)), ((), ()))


def dot(a, b, dims=(((1,), (0,)), ((), ()))):
    return lax.dot_general(a, b, dims, preferred_element_type=F32)


def kernel(
    act_ref, grad_ref, wg_hbm, wu_hbm, wd_hbm,
    ig_ref, gg_hbm, ug_hbm, dg_hbm,
    xa, xb, acts, grads, wg, wu, wd, part, own_part, bsend, brecv, delta,
    total, own_total, ysend, yrecv, own_z, zsend, zrecv, gg, ug, dg,
    w_sem, o_sem, xa_recv, xb_recv, y0_recv, y_recv, b_recv, c_recv, dy_recv, dz_recv,
    xa_send, xb_send, y0_send, y_send, b_send, c_send, dy_send, dz_send,
):
    r = lax.axis_index("rows")
    zl = lax.axis_index("cols")
    dp = lax.axis_index("depth")
    y = lax.rem(dp, NY)
    z = lax.div(dp, NY) * ZLO + zl

    def row_peer(k):
        return {"rows": lax.rem(r + k, NR), "cols": zl, "depth": dp}

    def y_peer(k):
        return {"rows": r, "cols": zl, "depth": dp - y + lax.rem(y + k, NY)}

    def z_peer(k):
        t = lax.rem(z + (k + NZ), NZ)
        return {"rows": r, "cols": lax.rem(t, ZLO), "depth": lax.div(t, ZLO) * NY + y}

    def send(src, dst, ssem, rsem, dev):
        pltpu.make_async_remote_copy(
            src_ref=src, dst_ref=dst, send_sem=ssem, recv_sem=rsem,
            device_id=dev, device_id_type=pl.DeviceIdType.MESH,
        ).start()

    def drain(ref, sem):
        pltpu.make_async_copy(ref, ref, sem).wait()

    w_copies = [
        pltpu.make_async_copy(src, dst, w_sem.at[i])
        for i, (src, dst) in enumerate(((wg_hbm, wg), (wu_hbm, wu), (wd_hbm, wd)))
    ]
    for c in w_copies:
        c.start()

    mine = jnp.concatenate([act_ref[...].astype(F32), grad_ref[...].astype(F32)], axis=0).astype(BF)
    xa[0, y] = mine[:, :512]
    xb[0, y] = mine[:, 512:]

    barrier = pltpu.get_barrier_semaphore()
    peers = [row_peer(k) for k in range(1, NR)]
    peers += [y_peer(k) for k in range(1, NY)]
    peers += [z_peer(k) for k in range(1, NZ)]
    for p in peers:
        pl.semaphore_signal(barrier, inc=1, device_id=p, device_id_type=pl.DeviceIdType.MESH)
    pl.semaphore_wait(barrier, len(peers))

    def start_gather():
        for k in range(1, NY):
            send(xa.at[0, y], xa.at[0, y], y0_send, y0_recv, y_peer(k))
        send(xb.at[0, y], xb.at[1, y], xb_send.at[0], xb_recv.at[1], z_peer(1))
        send(xb.at[0, y], xb.at[2, y], xb_send.at[16], xb_recv.at[2], z_peer(-1))
        for k in range(1, NY):
            send(xb.at[0, y], xb.at[0, y], y_send.at[0], y_recv.at[0], y_peer(k))
        drain(xa.at[0, pl.ds(0, 3)], y0_recv)
        send(xa.at[0], xa.at[1], xa_send.at[0], xa_recv.at[1], z_peer(1))
        send(xa.at[0], xa.at[2], xa_send.at[16], xa_recv.at[2], z_peer(-1))

    def y_forward(slot):
        for k in range(1, NY):
            send(xb.at[slot, y], xb.at[slot, y], y_send.at[slot], y_recv.at[slot], y_peer(k))

    def gather_step(d):
        if d == 8:
            drain(xb.at[15, y], xb_recv.at[15])
            y_forward(15)
            drain(xa.at[15, pl.ds(0, 2)], xa_recv.at[15])
            drain(xa.at[15, pl.ds(2, 2)], xa_recv.at[16])
            return
        for slot, to in ((2 * d - 1, 1), (2 * d, -1)):
            drain(xb.at[slot, y], xb_recv.at[slot])
            if d < 7:
                send(xb.at[slot, y], xb.at[slot + 2, y], xb_send.at[slot], xb_recv.at[slot + 2], z_peer(to))
            elif to == -1:
                send(xb.at[slot, y], xb.at[15, y], xb_send.at[slot], xb_recv.at[15], z_peer(to))
            drain(xa.at[slot], xa_recv.at[slot])
            if d < 7:
                send(xa.at[slot], xa.at[slot + 2], xa_send.at[slot], xa_recv.at[slot + 2], z_peer(to))
            else:
                half = pl.ds(0, 2) if to == 1 else pl.ds(2, 2)
                send(xa.at[slot, half], xa.at[15, half], xa_send.at[slot],
                     xa_recv.at[15 if to == 1 else 16], z_peer(to))
            y_forward(slot)

    def partial_sums(c):
        for s in range(4 * c, 4 * c + 4):
            drain(xb.at[s, pl.ds(0, 3)], y_recv.at[s])

        def pick(p, carry):
            s = 4 * c + lax.div(p, 2)
            y0 = lax.rem(p, 2) * 2
            rows = pl.ds(pl.multiple_of(c * 128 + p * 16, 16), 16)
            for buf, cols in ((xa, pl.ds(0, 512)), (xb, pl.ds(512, 512))):
                b0 = buf[s, y0].astype(F32)
                b1 = buf[s, y0 + 1].astype(F32)
                acts[rows, cols] = jnp.concatenate([b0[:8], b1[:8]], axis=0).astype(BF)
                grads[rows, cols] = jnp.concatenate([b0[8:], b1[8:]], axis=0).astype(BF)
            return carry

        lax.fori_loop(0, 8, pick, 0)
        rows = pl.ds(c * 128, 128)
        part[:, 0:256] = dot(acts[rows], wg[...])
        part[:, 256:512] = dot(acts[rows], wu[...])
        part[:, 512:768] = dot(grads[rows], wd[...], NT)
        bsend[c] = part[...].astype(BF).reshape(NR, 16, 768)
        own_part[c] = part[pl.ds(pl.multiple_of(r * 16, 16), 16)]
        for k in range(1, NR):
            send(bsend.at[c, lax.rem(r + k, NR)], brecv.at[c, k - 1], b_send.at[c], b_recv.at[c], row_peer(k))

    def pointwise(c):
        drain(brecv.at[c], b_recv.at[c])
        tot = own_part[c]
        for k in range(NR - 1):
            tot = tot + brecv[c, k].astype(F32)
        gate, up, hid = tot[:, 0:256], tot[:, 256:512], tot[:, 512:768]
        sig = 1.0 / (1.0 + jnp.exp(-gate))
        delta[c, r, :, 0:256] = (gate * sig * up).astype(BF)
        delta[c, r, :, 256:512] = (hid * up * sig * (1.0 + gate * (1.0 - sig))).astype(BF)
        delta[c, r, :, 512:768] = (hid * gate * sig).astype(BF)
        for k in range(1, NR):
            send(delta.at[c, r], delta.at[c, r], c_send.at[c], c_recv.at[c], row_peer(k))

    def input_terms(c):
        drain(delta.at[c, pl.ds(0, NR - 1)], c_recv.at[c])
        dl = delta[c].reshape(128, 768)
        total[...] = (dot(dl[:, 256:512], wg[...], NT) + dot(dl[:, 512:768], wu[...], NT)).reshape(4, NY, 8, 1024)
        for t in range(NY):
            ysend[c, t] = jnp.concatenate([total[s, t] for s in range(4)], axis=0).astype(BF)
        for s in range(4):
            own_total[c, s] = total[s, y]
        for k in range(1, NY):
            send(ysend.at[c, lax.rem(y + k, NY)], yrecv.at[c, k - 1], dy_send.at[c], dy_recv.at[c], y_peer(k))

    def slot_offset(slot):
        return -((slot + 1) // 2) if slot % 2 else slot // 2

    def reduce_y(c):
        drain(yrecv.at[c], dy_recv.at[c])
        for s in range(4):
            slot = 4 * c + s
            if s % 2 == 0:
                got = [yrecv[c, k, 8 * s:8 * s + 16, :].astype(F32) for k in range(NY - 1)]
            lo = 8 * (s % 2)
            v = own_total[c, s] + (got[0][lo:lo + 8] + got[1][lo:lo + 8] + got[2][lo:lo + 8])
            v = jnp.concatenate([v[:, :512], v[:, 512:]], axis=0)
            if slot == 0:
                own_z[...] = v
            else:
                zsend[slot - 1] = v.astype(BF)
        for s in range(4):
            slot = 4 * c + s
            if slot:
                k = slot_offset(slot) % NZ
                send(zsend.at[slot - 1], zrecv.at[k - 1], dz_send, dz_recv, z_peer(k))

    def reduce_z():
        drain(zrecv, dz_recv)
        v = own_z[...]
        for k in range(NZ - 1):
            v = v + zrecv[k].astype(F32)
        ig_ref[...] = jnp.concatenate([v[:8], v[8:]], axis=1).astype(BF)

    def weight_grads():
        dl = delta[...].reshape(512, 768)
        gg[...] = dot(acts[...], dl[:, 256:512], TN).astype(BF)
        ug[...] = dot(acts[...], dl[:, 512:768], TN).astype(BF)
        dg[...] = dot(dl[:, 0:256], grads[...], TN).astype(BF)

    out_copies = [
        pltpu.make_async_copy(src, dst, o_sem.at[i])
        for i, (src, dst) in enumerate(((gg, gg_hbm), (ug, ug_hbm), (dg, dg_hbm)))
    ]

    start_gather()
    gather_step(1)
    for c in w_copies:
        c.wait()
    gather_step(2)
    partial_sums(0)
    gather_step(3)
    pointwise(0)
    gather_step(4)
    partial_sums(1)
    input_terms(0)
    gather_step(5)
    pointwise(1)
    reduce_y(0)
    gather_step(6)
    partial_sums(2)
    input_terms(1)
    gather_step(7)
    pointwise(2)
    reduce_y(1)
    gather_step(8)
    partial_sums(3)
    input_terms(2)
    pointwise(3)
    reduce_y(2)
    input_terms(3)
    weight_grads()
    for c in out_copies:
        c.start()
    reduce_y(3)
    reduce_z()

    drain(xa.at[0, pl.ds(0, 3)], y0_send)
    for s in (0, 16, *range(1, 13)):
        drain(xa.at[min(s, 15)], xa_send.at[s])
    for s in (13, 14):
        drain(xa.at[s, pl.ds(0, 2)], xa_send.at[s])
    for s in (0, 16, *range(1, 13), 14):
        drain(xb.at[min(s, 15), 0], xb_send.at[s])
    for s in range(16):
        drain(xb.at[s, pl.ds(0, 3)], y_send.at[s])
    for c in range(CHUNKS):
        drain(brecv.at[c], b_send.at[c])
        drain(delta.at[c, pl.ds(0, NR - 1)], c_send.at[c])
        drain(yrecv.at[c], dy_send.at[c])
    drain(zsend, dz_send)
    for c in out_copies:
        c.wait()


def body(activations, out_grad, w_gate, w_up, w_down):
    vmem = pl.BlockSpec(memory_space=pltpu.VMEM)
    hbm = pl.BlockSpec(memory_space=pl.ANY)
    dma = pltpu.SemaphoreType.DMA
    return pl.pallas_call(
        kernel,
        out_shape=(
            jax.ShapeDtypeStruct((8, 1024), BF),
            jax.ShapeDtypeStruct((1024, 256), BF),
            jax.ShapeDtypeStruct((1024, 256), BF),
            jax.ShapeDtypeStruct((256, 1024), BF),
        ),
        in_specs=[vmem, vmem, hbm, hbm, hbm],
        out_specs=(vmem, hbm, hbm, hbm),
        scratch_shapes=[
            pltpu.VMEM((16, 4, 16, 512), BF),
            pltpu.VMEM((16, 4, 16, 512), BF),
            pltpu.VMEM((512, 1024), BF),
            pltpu.VMEM((512, 1024), BF),
            pltpu.VMEM((1024, 256), BF),
            pltpu.VMEM((1024, 256), BF),
            pltpu.VMEM((256, 1024), BF),
            pltpu.VMEM((128, 768), F32),
            pltpu.VMEM((CHUNKS, 16, 768), F32),
            pltpu.VMEM((CHUNKS, NR, 16, 768), BF),
            pltpu.VMEM((CHUNKS, NR - 1, 16, 768), BF),
            pltpu.VMEM((CHUNKS, NR, 16, 768), BF),
            pltpu.VMEM((4, NY, 8, 1024), F32),
            pltpu.VMEM((CHUNKS, 4, 8, 1024), F32),
            pltpu.VMEM((CHUNKS, NY, 32, 1024), BF),
            pltpu.VMEM((CHUNKS, NY - 1, 32, 1024), BF),
            pltpu.VMEM((16, 512), F32),
            pltpu.VMEM((NZ - 1, 16, 512), BF),
            pltpu.VMEM((NZ - 1, 16, 512), BF),
            pltpu.VMEM((1024, 256), BF),
            pltpu.VMEM((1024, 256), BF),
            pltpu.VMEM((256, 1024), BF),
            dma((3,)), dma((3,)),
            dma((17,)), dma((17,)), dma, dma((16,)), dma((CHUNKS,)), dma((CHUNKS,)), dma((CHUNKS,)), dma,
            dma((17,)), dma((17,)), dma, dma((16,)), dma((CHUNKS,)), dma((CHUNKS,)), dma((CHUNKS,)), dma,
        ],
        compiler_params=pltpu.CompilerParams(
            collective_id=0, has_side_effects=True, vmem_limit_bytes=48 * 1024 * 1024
        ),
        cost_estimate=pl.CostEstimate(flops=2200000000, bytes_accessed=3200000, transcendentals=16384),
    )(activations, out_grad, w_gate, w_up, w_down)


def solution(mesh):
    in_specs = (
        P(("cols", "depth"), "rows"),
        P(("cols", "depth"), "rows"),
        P("rows", ("cols", "depth")),
        P("rows", ("cols", "depth")),
        P(("cols", "depth"), "rows"),
    )
    out_specs = (
        P(("cols", "depth"), "rows"),
        P("rows", ("cols", "depth")),
        P("rows", ("cols", "depth")),
        P(("cols", "depth"), "rows"),
    )
    return jax.shard_map(body, mesh=mesh, in_specs=in_specs, out_specs=out_specs, check_vma=False)
```

time: 1610 us -> 98.9 us (0.06)
  the two profiles are of different devices: /device:TPU:24 before, /device:TPU:1 now
where the time goes in v1:
time: 98.9 us; the launch traced here: 98.6 us
  Pallas kernels  90.4 us (91%)
  local copies, waits for them, and re-layouts  7.54 us (8%)
    pallas_call x1, Pallas kernels, body(): pl.pallas_call(kernel, out_shape=(jax.ShapeDtypeStruct((8, 1024), BF), ja...  90.4 us
    unnamed x14, local copies, waits for them, and re-layouts  7.54 us

profile of v1, /device:TPU:1, one launch (start us, length us, event | category | flops | bytes accessed | tf_op | source)
XLA Modules:
  0.0 98.6 jit_solution(2761830622457032878)
XLA Ops:
  0.6 0.0 copy-start
  0.6 1.0 %copy-done = bf16[1024,256]{1,0:T(8,128)(2,1)S(1)} copy-done((bf16[1024,256]{1,0:T(8,128)(2,1)S(1)}, bf16[1024,256]{1,0:T(8,128)(2,1)}, u32[]{:S(2)}) %copy-start) | copy-done | bytes 524312
  1.7 0.0 copy-start.1
  1.7 1.0 %copy-done.1 = bf16[1024,256]{1,0:T(8,128)(2,1)S(1)} copy-done((bf16[1024,256]{1,0:T(8,128)(2,1)S(1)}, bf16[1024,256]{1,0:T(8,128)(2,1)}, u32[]{:S(2)}) %copy-start.1) | copy-done | bytes 524312
  2.7 0.0 copy-start.2
  2.7 1.0 %copy-done.2 = bf16[256,1024]{1,0:T(8,128)(2,1)S(1)} copy-done((bf16[256,1024]{1,0:T(8,128)(2,1)S(1)}, bf16[256,1024]{1,0:T(8,128)(2,1)}, u32[]{:S(2)}) %copy-start.2) | copy-done | bytes 524312
  3.8 0.0 copy-start.3
  3.8 0.7 copy-done.3
  4.5 0.0 copy-start.4
  4.5 0.7 copy-done.4
  5.2 90.4 %shard_map.84 = (bf16[8,1024]{1,0:T(8,128)(2,1)S(1)}, bf16[1024,256]{1,0:T(8,128)(2,1)S(1)}, bf16[1024,256]{1,0:T(8,128)(2,1)S(1)}, bf16[256,1024]{1,0:T(8,128)(2,1)S(1)}) custom-call(bf16[8,1024]{1,0:T(8,128)(2,1)S(1)} %copy-done.3, bf16[8,1024]{1,0:T(8,128)(2,1)S(1)} %copy-done.4, bf16[1024,256]{1,0:T(8,128)(2,1)S(1)} %copy-done, ...), custom_call_target="tpu_custom_call" | custom-call | flops 2200000000 | bytes 3200000 | tf_op jit(solution)/shard_map/pallas_call | solution.py:252
  95.6 0.6 copy.13
  96.2 0.8 copy.14
  97.0 0.8 copy.15
  97.8 0.8 copy.16
Async XLA Ops:
  0.6 1.0 %copy-start = (bf16[1024,256]{1,0:T(8,128)(2,1)S(1)}, bf16[1024,256]{1,0:T(8,128)(2,1)}, u32[]{:S(2)}) copy-start(bf16[1024,256]{1,0:T(8,128)(2,1)} %wg_hbm.1) | copy-start | bytes 1572868
  1.7 1.0 %copy-start.1 = (bf16[1024,256]{1,0:T(8,128)(2,1)S(1)}, bf16[1024,256]{1,0:T(8,128)(2,1)}, u32[]{:S(2)}) copy-start(bf16[1024,256]{1,0:T(8,128)(2,1)} %wu_hbm.1) | copy-start | bytes 1572868
  2.7 1.0 %copy-start.2 = (bf16[256,1024]{1,0:T(8,128)(2,1)S(1)}, bf16[256,1024]{1,0:T(8,128)(2,1)}, u32[]{:S(2)}) copy-start(bf16[256,1024]{1,0:T(8,128)(2,1)} %wd_hbm.1) | copy-start | bytes 1572868
  3.8 0.7 copy-start.3
  4.5 0.7 copy-start.4

commit v2 on v1

--- a/solution.py
+++ b/solution.py
@@ -9,19 +9,29 @@
 F32 = jnp.float32
 NR, NY, NZ, ZLO = 8, 4, 16, 8
 CHUNKS = 4
+OWN = 15
+WA = 256
 NT = (((1,), (1,)), ((), ()))
 TN = (((0,), (0,)), ((), ()))
 
 
+ORDER = (
+    ("relay_b", 0), ("relay_a", 0), ("relay_b", 1), ("partial", 0), ("relay_a", 1), ("relay_b", 2), ("relay_a", 2),
+    ("partial", 1), ("point", 0), ("relay_b", 3), ("partial", 2), ("point", 1), ("terms", 0), ("partial", 3),
+    ("point", 2), ("terms", 1), ("reduce", 0), ("point", 3), ("terms", 2), ("reduce", 1), ("terms", 3), ("grads", 0),
+    ("reduce", 2), ("reduce", 3),
+)
+
+
 def dot(a, b, dims=(((1,), (0,)), ((), ()))):
     return lax.dot_general(a, b, dims, preferred_element_type=F32)
 
 
 def kernel(
     act_ref, grad_ref, wg_hbm, wu_hbm, wd_hbm,
-    ig_ref, gg_hbm, ug_hbm, dg_hbm,
+    ig_hbm, gg_hbm, ug_hbm, dg_hbm,
     xa, xb, acts, grads, wg, wu, wd, part, own_part, bsend, brecv, delta,
-    total, own_total, ysend, yrecv, own_z, zsend, zrecv, gg, ug, dg,
+    total, own_total, ysend, yrecv, own_z, zsend, zrecv, ig, gg, ug, dg,
     w_sem, o_sem, xa_recv, xb_recv, y0_recv, y_recv, b_recv, c_recv, dy_recv, dz_recv,
     xa_send, xb_send, y0_send, y_send, b_send, c_send, dy_send, dz_send,
 ):
@@ -58,8 +68,8 @@
         c.start()
 
     mine = jnp.concatenate([act_ref[...].astype(F32), grad_ref[...].astype(F32)], axis=0).astype(BF)
-    xa[0, y] = mine[:, :512]
-    xb[0, y] = mine[:, 512:]
+    xa[OWN, y] = mine[:, :WA]
+    xb[OWN, y] = mine[:, WA:]
 
     barrier = pltpu.get_barrier_semaphore()
     peers = [row_peer(k) for k in range(1, NR)]
@@ -69,52 +79,69 @@
         pl.semaphore_signal(barrier, inc=1, device_id=p, device_id_type=pl.DeviceIdType.MESH)
     pl.semaphore_wait(barrier, len(peers))
 
-    def start_gather():
-        for k in range(1, NY):
-            send(xa.at[0, y], xa.at[0, y], y0_send, y0_recv, y_peer(k))
-        send(xb.at[0, y], xb.at[1, y], xb_send.at[0], xb_recv.at[1], z_peer(1))
-        send(xb.at[0, y], xb.at[2, y], xb_send.at[16], xb_recv.at[2], z_peer(-1))
-        for k in range(1, NY):
-            send(xb.at[0, y], xb.at[0, y], y_send.at[0], y_recv.at[0], y_peer(k))
-        drain(xa.at[0, pl.ds(0, 3)], y0_recv)
-        send(xa.at[0], xa.at[1], xa_send.at[0], xa_recv.at[1], z_peer(1))
-        send(xa.at[0], xa.at[2], xa_send.at[16], xa_recv.at[2], z_peer(-1))
-
     def y_forward(slot):
         for k in range(1, NY):
             send(xb.at[slot, y], xb.at[slot, y], y_send.at[slot], y_recv.at[slot], y_peer(k))
 
-    def gather_step(d):
-        if d == 8:
-            drain(xb.at[15, y], xb_recv.at[15])
-            y_forward(15)
-            drain(xa.at[15, pl.ds(0, 2)], xa_recv.at[15])
-            drain(xa.at[15, pl.ds(2, 2)], xa_recv.at[16])
+    def start_gather():
+        for k in range(1, NY):
+            send(xa.at[OWN, y], xa.at[OWN, y], y0_send, y0_recv, y_peer(k))
+        for to, k in ((2, 2), (3, -2), (0, 1), (1, -1)):
+            send(xb.at[OWN, y], xb.at[to, y], xb_send.at[OWN], xb_recv.at[to], z_peer(k))
+        y_forward(OWN)
+        drain(xa.at[OWN, pl.ds(0, 3)], y0_recv)
+        for to, k in ((2, 2), (3, -2), (0, 1), (1, -1)):
+            send(xa.at[OWN], xa.at[to], xa_send.at[OWN], xa_recv.at[to], z_peer(k))
+
+    def relay_b(c):
+        if c == 3:
+            for slot in (12, 13, 14):
+                drain(xb.at[slot, y], xb_recv.at[slot])
+                y_forward(slot)
             return
-        for slot, to in ((2 * d - 1, 1), (2 * d, -1)):
+        for slot in (4 * c, 4 * c + 1):
             drain(xb.at[slot, y], xb_recv.at[slot])
-            if d < 7:
-                send(xb.at[slot, y], xb.at[slot + 2, y], xb_send.at[slot], xb_recv.at[slot + 2], z_peer(to))
-            elif to == -1:
-                send(xb.at[slot, y], xb.at[15, y], xb_send.at[slot], xb_recv.at[15], z_peer(to))
+            y_forward(slot)
+        for slot, sign in ((4 * c + 2, 1), (4 * c + 3, -1)):
+            drain(xb.at[slot, y], xb_recv.at[slot])
+            if c < 2:
+                send(xb.at[slot, y], xb.at[slot + 4, y], xb_send.at[slot], xb_recv.at[slot + 4], z_peer(2 * sign))
+            elif sign == -1:
+                send(xb.at[slot, y], xb.at[14, y], xb_send.at[slot], xb_recv.at[14], z_peer(-2))
+            send(xb.at[slot, y], xb.at[slot + 2, y], xb_send.at[slot], xb_recv.at[slot + 2], z_peer(sign))
+            y_forward(slot)
+
+    def relay_a(c):
+        for slot, sign in ((4 * c + 2, 1), (4 * c + 3, -1)):
             drain(xa.at[slot], xa_recv.at[slot])
-            if d < 7:
-                send(xa.at[slot], xa.at[slot + 2], xa_send.at[slot], xa_recv.at[slot + 2], z_peer(to))
+            if c < 2:
+                send(xa.at[slot], xa.at[slot + 4], xa_send.at[slot], xa_recv.at[slot + 4], z_peer(2 * sign))
             else:
-                half = pl.ds(0, 2) if to == 1 else pl.ds(2, 2)
-                send(xa.at[slot, half], xa.at[15, half], xa_send.at[slot],
-                     xa_recv.at[15 if to == 1 else 16], z_peer(to))
-            y_forward(slot)
-
-    def partial_sums(c):
+                half = pl.ds(0, 2) if sign == 1 else pl.ds(2, 2)
+                extra = 16 if sign == 1 else 17
+                send(xa.at[slot, half], xa.at[14, half], xa_send.at[extra], xa_recv.at[extra], z_peer(2 * sign))
+            send(xa.at[slot], xa.at[slot + 2], xa_send.at[slot], xa_recv.at[slot + 2], z_peer(sign))
+
+    def gather_wait(c):
         for s in range(4 * c, 4 * c + 4):
             drain(xb.at[s, pl.ds(0, 3)], y_recv.at[s])
+        if c < 3:
+            for s in (4 * c, 4 * c + 1):
+                drain(xa.at[s], xa_recv.at[s])
+        else:
+            for s in (12, 13):
+                drain(xa.at[s], xa_recv.at[s])
+            drain(xa.at[14, pl.ds(0, 2)], xa_recv.at[16])
+            drain(xa.at[14, pl.ds(2, 2)], xa_recv.at[17])
+
+    def partial_sums(c):
+        gather_wait(c)
 
         def pick(p, carry):
             s = 4 * c + lax.div(p, 2)
             y0 = lax.rem(p, 2) * 2
             rows = pl.ds(pl.multiple_of(c * 128 + p * 16, 16), 16)
-            for buf, cols in ((xa, pl.ds(0, 512)), (xb, pl.ds(512, 512))):
+            for buf, cols in ((xa, pl.ds(0, WA)), (xb, pl.ds(WA, 1024 - WA))):
                 b0 = buf[s, y0].astype(F32)
                 b1 = buf[s, y0 + 1].astype(F32)
                 acts[rows, cols] = jnp.concatenate([b0[:8], b1[:8]], axis=0).astype(BF)
@@ -156,7 +183,10 @@
             send(ysend.at[c, lax.rem(y + k, NY)], yrecv.at[c, k - 1], dy_send.at[c], dy_recv.at[c], y_peer(k))
 
     def slot_offset(slot):
-        return -((slot + 1) // 2) if slot % 2 else slot // 2
+        if slot == 14:
+            return 8
+        c, s = divmod(slot, 4)
+        return (2 * c + 1 + s // 2) * (1 if s % 2 else -1)
 
     def reduce_y(c):
         drain(yrecv.at[c], dy_recv.at[c])
@@ -167,22 +197,22 @@
             lo = 8 * (s % 2)
             v = own_total[c, s] + (got[0][lo:lo + 8] + got[1][lo:lo + 8] + got[2][lo:lo + 8])
             v = jnp.concatenate([v[:, :512], v[:, 512:]], axis=0)
-            if slot == 0:
+            if slot == OWN:
                 own_z[...] = v
             else:
-                zsend[slot - 1] = v.astype(BF)
+                zsend[slot] = v.astype(BF)
         for s in range(4):
             slot = 4 * c + s
-            if slot:
+            if slot != OWN:
                 k = slot_offset(slot) % NZ
-                send(zsend.at[slot - 1], zrecv.at[k - 1], dz_send, dz_recv, z_peer(k))
+                send(zsend.at[slot], zrecv.at[k - 1], dz_send, dz_recv, z_peer(k))
 
     def reduce_z():
         drain(zrecv, dz_recv)
         v = own_z[...]
         for k in range(NZ - 1):
             v = v + zrecv[k].astype(F32)
-        ig_ref[...] = jnp.concatenate([v[:8], v[8:]], axis=1).astype(BF)
+        ig[...] = jnp.concatenate([v[:8], v[8:]], axis=1).astype(BF)
 
     def weight_grads():
         dl = delta[...].reshape(512, 768)
@@ -196,60 +226,75 @@
     ]
 
     start_gather()
-    gather_step(1)
     for c in w_copies:
         c.wait()
-    gather_step(2)
-    partial_sums(0)
-    gather_step(3)
-    pointwise(0)
-    gather_step(4)
-    partial_sums(1)
-    input_terms(0)
-    gather_step(5)
-    pointwise(1)
-    reduce_y(0)
-    gather_step(6)
-    partial_sums(2)
-    input_terms(1)
-    gather_step(7)
-    pointwise(2)
-    reduce_y(1)
-    gather_step(8)
-    partial_sums(3)
-    input_terms(2)
-    pointwise(3)
-    reduce_y(2)
-    input_terms(3)
-    weight_grads()
-    for c in out_copies:
-        c.start()
-    reduce_y(3)
-    reduce_z()
-
+    for stage, c in ORDER:
+        if stage == "grads":
+            weight_grads()
+            for copy in out_copies:
+                copy.start()
+        else:
+            {"relay_b": relay_b, "relay_a": relay_a, "partial": partial_sums, "point": pointwise,
+             "terms": input_terms, "reduce": reduce_y}[stage](c)
     drain(xa.at[0, pl.ds(0, 3)], y0_send)
-    for s in (0, 16, *range(1, 13)):
-        drain(xa.at[min(s, 15)], xa_send.at[s])
-    for s in (13, 14):
-        drain(xa.at[s, pl.ds(0, 2)], xa_send.at[s])
-    for s in (0, 16, *range(1, 13), 14):
-        drain(xb.at[min(s, 15), 0], xb_send.at[s])
+    drain(xa.at[pl.ds(0, 4)], xa_send.at[OWN])
+    drain(xb.at[0], xb_send.at[OWN])
+    for s in (2, 3, 6, 7):
+        drain(xa.at[pl.ds(0, 2)], xa_send.at[s])
+        drain(xb.at[0, pl.ds(0, 2)], xb_send.at[s])
+    for s in (10, 11):
+        drain(xa.at[0], xa_send.at[s])
+        drain(xb.at[0, pl.ds(0, s - 9)], xb_send.at[s])
+    for s in (16, 17):
+        drain(xa.at[0, pl.ds(0, 2)], xa_send.at[s])
     for s in range(16):
         drain(xb.at[s, pl.ds(0, 3)], y_send.at[s])
     for c in range(CHUNKS):
         drain(brecv.at[c], b_send.at[c])
         drain(delta.at[c, pl.ds(0, NR - 1)], c_send.at[c])
         drain(yrecv.at[c], dy_send.at[c])
-    drain(zsend, dz_send)
     for c in out_copies:
         c.wait()
+    reduce_z()
+    ig_copy = pltpu.make_async_copy(ig, ig_hbm, o_sem.at[3])
+    ig_copy.start()
+    drain(zsend, dz_send)
+    ig_copy.wait()
+
+
+def copy_kernel(*refs):
+    n = len(refs) // 3
+    ins, outs, bufs, sems = refs[:n], refs[n:2 * n], refs[2 * n:3 * n], refs[3 * n]
+    loads = [pltpu.make_async_copy(ins[i], bufs[i], sems.at[0, i]) for i in range(n)]
+    stores = [pltpu.make_async_copy(bufs[i], outs[i], sems.at[1, i]) for i in range(n)]
+    for c in loads:
+        c.start()
+    for load, store in zip(loads, stores):
+        load.wait()
+        store.start()
+    for c in stores:
+        c.wait()
+
+
+def write_out(*arrays):
+    hbm = pl.BlockSpec(memory_space=pltpu.HBM)
+    return pl.pallas_call(
+        copy_kernel,
+        out_shape=tuple(jax.ShapeDtypeStruct(a.shape, a.dtype) for a in arrays),
+        in_specs=[pl.BlockSpec(memory_space=pl.ANY)] * len(arrays),
+        out_specs=(hbm,) * len(arrays),
+        scratch_shapes=[pltpu.VMEM(a.shape, a.dtype) for a in arrays]
+        + [pltpu.SemaphoreType.DMA((2, len(arrays)))],
+        compiler_params=pltpu.CompilerParams(vmem_limit_bytes=60 * 1024 * 1024),
+    )(*arrays)
 
 
 def body(activations, out_grad, w_gate, w_up, w_down):
     vmem = pl.BlockSpec(memory_space=pltpu.VMEM)
-    hbm = pl.BlockSpec(memory_space=pl.ANY)
+    hbm = pl.BlockSpec(memory_space=pltpu.HBM)
+    any_space = pl.BlockSpec(memory_space=pl.ANY)
     dma = pltpu.SemaphoreType.DMA
-    return pl.pallas_call(
+    outs = pl.pallas_call(
         kernel,
         out_shape=(
             jax.ShapeDtypeStruct((8, 1024), BF),
@@ -258,10 +303,10 @@
             jax.ShapeDtypeStruct((256, 1024), BF),
         ),
         in_specs=[vmem, vmem, hbm, hbm, hbm],
-        out_specs=(vmem, hbm, hbm, hbm),
+        out_specs=(any_space, any_space, any_space, any_space),
         scratch_shapes=[
-            pltpu.VMEM((16, 4, 16, 512), BF),
-            pltpu.VMEM((16, 4, 16, 512), BF),
+            pltpu.VMEM((16, 4, 16, WA), BF),
+            pltpu.VMEM((16, 4, 16, 1024 - WA), BF),
             pltpu.VMEM((512, 1024), BF),
             pltpu.VMEM((512, 1024), BF),
             pltpu.VMEM((1024, 256), BF),
@@ -279,18 +324,20 @@
             pltpu.VMEM((16, 512), F32),
             pltpu.VMEM((NZ - 1, 16, 512), BF),
             pltpu.VMEM((NZ - 1, 16, 512), BF),
+            pltpu.VMEM((8, 1024), BF),
             pltpu.VMEM((1024, 256), BF),
             pltpu.VMEM((1024, 256), BF),
             pltpu.VMEM((256, 1024), BF),
-            dma((3,)), dma((3,)),
-            dma((17,)), dma((17,)), dma, dma((16,)), dma((CHUNKS,)), dma((CHUNKS,)), dma((CHUNKS,)), dma,
-            dma((17,)), dma((17,)), dma, dma((16,)), dma((CHUNKS,)), dma((CHUNKS,)), dma((CHUNKS,)), dma,
+            dma((3,)), dma((4,)),
+            dma((18,)), dma((16,)), dma, dma((16,)), dma((CHUNKS,)), dma((CHUNKS,)), dma((CHUNKS,)), dma,
+            dma((18,)), dma((16,)), dma, dma((16,)), dma((CHUNKS,)), dma((CHUNKS,)), dma((CHUNKS,)), dma,
         ],
         compiler_params=pltpu.CompilerParams(
-            collective_id=0, has_side_effects=True, vmem_limit_bytes=48 * 1024 * 1024
+            collective_id=0, has_side_effects=True, vmem_limit_bytes=60 * 1024 * 1024
         ),
         cost_estimate=pl.CostEstimate(flops=2200000000, bytes_accessed=3200000, transcendentals=16384),
     )(activations, out_grad, w_gate, w_up, w_down)
+    return write_out(*outs)
 
 
 def solution(mesh):

time: 98.9 us -> 73.1 us (0.74)
  Pallas kernels: 90.4 us -> 72.1 us
  local copies, waits for them, and re-layouts: 7.54 us -> 0 us
    pallas_call x1, Pallas kernels: 90.4 us -> 69.8 us  [body(): pl.pallas_call(kernel, out_shape=(jax.ShapeDtypeStruct((8, 1024), BF), ja...]
    unnamed x14 -> x0, local copies, waits for them, and re-layouts: 7.54 us -> none
    pallas_call x0 -> x1, Pallas kernels: none -> 2.27 us  [write_out(): pl.pallas_call(copy_kernel, out_shape=tuple((jax.ShapeDtypeStruct(a.shape...]
where the time goes in v2:
time: 73.1 us; the launch traced here: 72.7 us
  Pallas kernels  72.1 us (99%)
    pallas_call x1, Pallas kernels, body(): pl.pallas_call(kernel, out_shape=(jax.ShapeDtypeStruct((8, 1024), BF), ja...  69.8 us
    pallas_call x1, Pallas kernels, write_out(): pl.pallas_call(copy_kernel, out_shape=tuple((jax.ShapeDtypeStruct(a.shape...  2.27 us

profile of v2, /device:TPU:1, one launch (start us, length us, event | category | flops | bytes accessed | tf_op | source)
XLA Modules:
  0.0 72.7 jit_solution(17692643873213385732)
XLA Ops:
  0.6 69.8 %shard_map.84 = (bf16[8,1024]{1,0:T(8,128)(2,1)}, bf16[1024,256]{1,0:T(8,128)(2,1)}, bf16[1024,256]{1,0:T(8,128)(2,1)}, bf16[256,1024]{1,0:T(8,128)(2,1)}) custom-call(bf16[8,1024]{1,0:T(8,128)(2,1)} %act_ref.1, bf16[8,1024]{1,0:T(8,128)(2,1)} %grad_ref.1, bf16[1024,256]{1,0:T(8,128)(2,1)} %wg_hbm.1, bf16[1024,256]{1,0:T(8,128)(2,1)} %wu_hbm.1, ...), custom_call_target="tpu_custom_call" | custom-call | flops 2200000000 | bytes 3200000 | tf_op jit(solution)/shard_map/pallas_call | solution.py:297
  70.5 2.3 %shard_map.85 = (bf16[8,1024]{1,0:T(8,128)(2,1)}, bf16[1024,256]{1,0:T(8,128)(2,1)}, bf16[1024,256]{1,0:T(8,128)(2,1)}, bf16[256,1024]{1,0:T(8,128)(2,1)}) custom-call(bf16[8,1024]{1,0:T(8,128)(2,1)} %get-tuple-element.8.refs_0_, bf16[1024,256]{1,0:T(8,128)(2,1)} %get-tuple-element.9.refs_1_, bf16[1024,256]{1,0:T(8,128)(2,1)} %get-tuple-element.10.refs_2_, ...), custom_call_target="tpu_custom_call" | custom-call | tf_op jit(solution)/shard_map/pallas_call | solution.py:281

commit v3 on v2

--- a/solution.py
+++ b/solution.py
@@ -8,7 +8,7 @@
 BF = jnp.bfloat16
 F32 = jnp.float32
 NR, NY, NZ, ZLO = 8, 4, 16, 8
-CHUNKS = 4
+CHUNKS = 8
 OWN = 15
 WA = 256
 NT = (((1,), (1,)), ((), ()))
@@ -16,10 +16,13 @@
 
 
 ORDER = (
-    ("relay_b", 0), ("relay_a", 0), ("relay_b", 1), ("partial", 0), ("relay_a", 1), ("relay_b", 2), ("relay_a", 2),
-    ("partial", 1), ("point", 0), ("relay_b", 3), ("partial", 2), ("point", 1), ("terms", 0), ("partial", 3),
-    ("point", 2), ("terms", 1), ("reduce", 0), ("point", 3), ("terms", 2), ("reduce", 1), ("terms", 3), ("grads", 0),
-    ("reduce", 2), ("reduce", 3),
+    ("relay_b", 0), ("relay_a", 0), ("relay_b", 1), ("partial", 0), ("relay_a", 1), ("partial", 1),
+    ("relay_b", 2), ("relay_a", 2), ("partial", 2), ("point", 0), ("partial", 3), ("point", 1),
+    ("relay_b", 3), ("partial", 4), ("point", 2), ("terms", 0), ("partial", 5), ("point", 3),
+    ("terms", 1), ("partial", 6), ("point", 4), ("terms", 2), ("reduce", 0), ("partial", 7),
+    ("point", 5), ("terms", 3), ("reduce", 1), ("point", 6), ("terms", 4), ("reduce", 2),
+    ("point", 7), ("terms", 5), ("reduce", 3), ("terms", 6), ("reduce", 4), ("terms", 7),
+    ("reduce", 5), ("grads", 0), ("reduce", 6), ("reduce", 7),
 )
 
 
@@ -30,7 +33,7 @@
 def kernel(
     act_ref, grad_ref, wg_hbm, wu_hbm, wd_hbm,
     ig_hbm, gg_hbm, ug_hbm, dg_hbm,
-    xa, xb, acts, grads, wg, wu, wd, part, own_part, bsend, brecv, delta,
+    xa, xb, acts, grads, wg, wu, wd, part, own_part, bsend, brecv, delta, deltas,
     total, own_total, ysend, yrecv, own_z, zsend, zrecv, ig, gg, ug, dg,
     w_sem, o_sem, xa_recv, xb_recv, y0_recv, y_recv, b_recv, c_recv, dy_recv, dz_recv,
     xa_send, xb_send, y0_send, y_send, b_send, c_send, dy_send, dz_send,
@@ -123,14 +126,11 @@
             send(xa.at[slot], xa.at[slot + 2], xa_send.at[slot], xa_recv.at[slot + 2], z_peer(sign))
 
     def gather_wait(c):
-        for s in range(4 * c, 4 * c + 4):
+        for s in (2 * c, 2 * c + 1):
             drain(xb.at[s, pl.ds(0, 3)], y_recv.at[s])
-        if c < 3:
-            for s in (4 * c, 4 * c + 1):
+            if c % 2 == 0:
                 drain(xa.at[s], xa_recv.at[s])
-        else:
-            for s in (12, 13):
-                drain(xa.at[s], xa_recv.at[s])
+        if c == 7:
             drain(xa.at[14, pl.ds(0, 2)], xa_recv.at[16])
             drain(xa.at[14, pl.ds(2, 2)], xa_recv.at[17])
 
@@ -138,9 +138,9 @@
         gather_wait(c)
 
         def pick(p, carry):
-            s = 4 * c + lax.div(p, 2)
+            s = 2 * c + lax.div(p, 2)
             y0 = lax.rem(p, 2) * 2
-            rows = pl.ds(pl.multiple_of(c * 128 + p * 16, 16), 16)
+            rows = pl.ds(pl.multiple_of(c * 64 + p * 16, 16), 16)
             for buf, cols in ((xa, pl.ds(0, WA)), (xb, pl.ds(WA, 1024 - WA))):
                 b0 = buf[s, y0].astype(F32)
                 b1 = buf[s, y0 + 1].astype(F32)
@@ -148,36 +148,49 @@
                 grads[rows, cols] = jnp.concatenate([b0[8:], b1[8:]], axis=0).astype(BF)
             return carry
 
-        lax.fori_loop(0, 8, pick, 0)
-        rows = pl.ds(c * 128, 128)
+        lax.fori_loop(0, 4, pick, 0)
+        rows = pl.ds(c * 64, 64)
         part[:, 0:256] = dot(acts[rows], wg[...])
         part[:, 256:512] = dot(acts[rows], wu[...])
         part[:, 512:768] = dot(grads[rows], wd[...], NT)
-        bsend[c] = part[...].astype(BF).reshape(NR, 16, 768)
-        own_part[c] = part[pl.ds(pl.multiple_of(r * 16, 16), 16)]
+        for k in range(NR):
+            v = part[8 * k:8 * k + 8, :]
+            bsend[c, k] = jnp.concatenate([v[:, :384], v[:, 384:]], axis=0).astype(BF)
+        own_part[c] = part[pl.ds(pl.multiple_of(r * 8, 8), 8)]
         for k in range(1, NR):
             send(bsend.at[c, lax.rem(r + k, NR)], brecv.at[c, k - 1], b_send.at[c], b_recv.at[c], row_peer(k))
 
     def pointwise(c):
         drain(brecv.at[c], b_recv.at[c])
         tot = own_part[c]
+        tot = jnp.concatenate([tot[:, :384], tot[:, 384:]], axis=0)
         for k in range(NR - 1):
             tot = tot + brecv[c, k].astype(F32)
+        tot = jnp.concatenate([tot[:8], tot[8:]], axis=1)
         gate, up, hid = tot[:, 0:256], tot[:, 256:512], tot[:, 512:768]
         sig = 1.0 / (1.0 + jnp.exp(-gate))
-        delta[c, r, :, 0:256] = (gate * sig * up).astype(BF)
-        delta[c, r, :, 256:512] = (hid * up * sig * (1.0 + gate * (1.0 - sig))).astype(BF)
-        delta[c, r, :, 512:768] = (hid * gate * sig).astype(BF)
+        hidden = gate * sig * up
+        gate_delta = hid * up * sig * (1.0 + gate * (1.0 - sig))
+        up_delta = hid * gate * sig
+        first = jnp.concatenate([hidden, gate_delta[:, :128]], axis=1)
+        second = jnp.concatenate([gate_delta[:, 128:], up_delta], axis=1)
+        delta[c, r] = jnp.concatenate([first, second], axis=0).astype(BF)
         for k in range(1, NR):
             send(delta.at[c, r], delta.at[c, r], c_send.at[c], c_recv.at[c], row_peer(k))
 
     def input_terms(c):
         drain(delta.at[c, pl.ds(0, NR - 1)], c_recv.at[c])
-        dl = delta[c].reshape(128, 768)
-        total[...] = (dot(dl[:, 256:512], wg[...], NT) + dot(dl[:, 512:768], wu[...], NT)).reshape(4, NY, 8, 1024)
-        for t in range(NY):
-            ysend[c, t] = jnp.concatenate([total[s, t] for s in range(4)], axis=0).astype(BF)
-        for s in range(4):
+        for k in range(0, NR, 2):
+            v0 = delta[c, k].astype(F32)
+            v1 = delta[c, k + 1].astype(F32)
+            rows = slice(c * 64 + 8 * k, c * 64 + 8 * k + 16)
+            deltas[rows, 0:384] = jnp.concatenate([v0[:8], v1[:8]], axis=0).astype(BF)
+            deltas[rows, 384:768] = jnp.concatenate([v0[8:], v1[8:]], axis=0).astype(BF)
+        dl = deltas[c * 64:c * 64 + 64, :]
+        total[...] = (dot(dl[:, 256:512], wg[...], NT) + dot(dl[:, 512:768], wu[...], NT)).reshape(2, NY, 8, 1024)
+        for k in range(NY):
+            ysend[c, k] = jnp.concatenate([total[0, k], total[1, k]], axis=0).astype(BF)
+        for s in range(2):
             own_total[c, s] = total[s, y]
         for k in range(1, NY):
             send(ysend.at[c, lax.rem(y + k, NY)], yrecv.at[c, k - 1], dy_send.at[c], dy_recv.at[c], y_peer(k))
@@ -185,25 +198,20 @@
     def slot_offset(slot):
         if slot == 14:
             return 8
-        c, s = divmod(slot, 4)
-        return (2 * c + 1 + s // 2) * (1 if s % 2 else -1)
+        return (slot // 2 + 1) * (1 if slot % 2 else -1)
 
     def reduce_y(c):
         drain(yrecv.at[c], dy_recv.at[c])
-        for s in range(4):
-            slot = 4 * c + s
-            if s % 2 == 0:
-                got = [yrecv[c, k, 8 * s:8 * s + 16, :].astype(F32) for k in range(NY - 1)]
-            lo = 8 * (s % 2)
+        got = [yrecv[c, k].astype(F32) for k in range(NY - 1)]
+        for s in range(2):
+            slot = 2 * c + s
+            lo = 8 * s
             v = own_total[c, s] + (got[0][lo:lo + 8] + got[1][lo:lo + 8] + got[2][lo:lo + 8])
             v = jnp.concatenate([v[:, :512], v[:, 512:]], axis=0)
             if slot == OWN:
                 own_z[...] = v
             else:
                 zsend[slot] = v.astype(BF)
-        for s in range(4):
-            slot = 4 * c + s
-            if slot != OWN:
                 k = slot_offset(slot) % NZ
                 send(zsend.at[slot], zrecv.at[k - 1], dz_send, dz_recv, z_peer(k))
 
@@ -215,7 +223,7 @@
         ig[...] = jnp.concatenate([v[:8], v[8:]], axis=1).astype(BF)
 
     def weight_grads():
-        dl = delta[...].reshape(512, 768)
+        dl = deltas[...]
         gg[...] = dot(acts[...], dl[:, 256:512], TN).astype(BF)
         ug[...] = dot(acts[...], dl[:, 512:768], TN).astype(BF)
         dg[...] = dot(dl[:, 0:256], grads[...], TN).astype(BF)
@@ -312,15 +320,16 @@
             pltpu.VMEM((1024, 256), BF),
             pltpu.VMEM((1024, 256), BF),
             pltpu.VMEM((256, 1024), BF),
-            pltpu.VMEM((128, 768), F32),
-            pltpu.VMEM((CHUNKS, 16, 768), F32),
-            pltpu.VMEM((CHUNKS, NR, 16, 768), BF),
-            pltpu.VMEM((CHUNKS, NR - 1, 16, 768), BF),
-            pltpu.VMEM((CHUNKS, NR, 16, 768), BF),
-            pltpu.VMEM((4, NY, 8, 1024), F32),
-            pltpu.VMEM((CHUNKS, 4, 8, 1024), F32),
-            pltpu.VMEM((CHUNKS, NY, 32, 1024), BF),
-            pltpu.VMEM((CHUNKS, NY - 1, 32, 1024), BF),
+            pltpu.VMEM((64, 768), F32),
+            pltpu.VMEM((CHUNKS, 8, 768), F32),
+            pltpu.VMEM((CHUNKS, NR, 16, 384), BF),
+            pltpu.VMEM((CHUNKS, NR - 1, 16, 384), BF),
+            pltpu.VMEM((CHUNKS, NR, 16, 384), BF),
+            pltpu.VMEM((512, 768), BF),
+            pltpu.VMEM((2, NY, 8, 1024), F32),
+            pltpu.VMEM((CHUNKS, 2, 8, 1024), F32),
+            pltpu.VMEM((CHUNKS, NY, 16, 1024), BF),
+            pltpu.VMEM((CHUNKS, NY - 1, 16, 1024), BF),
             pltpu.VMEM((16, 512), F32),
             pltpu.VMEM((NZ - 1, 16, 512), BF),
             pltpu.VMEM((NZ - 1, 16, 512), BF),

time: 73.1 us -> 69.2 us (0.947); the launches traced: 72.7 us -> 68 us
  Pallas kernels: 72.1 us -> 67.4 us
    pallas_call x1, Pallas kernels: 69.8 us -> 65.1 us  [body(): pl.pallas_call(kernel, out_shape=(jax.ShapeDtypeStruct((8, 1024), BF), ja...]
where the time goes in v3:
time: 69.2 us; the launch traced here: 68 us
  Pallas kernels  67.4 us (97%)
    pallas_call x1, Pallas kernels, body(): pl.pallas_call(kernel, out_shape=(jax.ShapeDtypeStruct((8, 1024), BF), ja...  65.1 us
    pallas_call x1, Pallas kernels, write_out(): pl.pallas_call(copy_kernel, out_shape=tuple((jax.ShapeDtypeStruct(a.shape...  2.27 us

profile of v3, /device:TPU:1, one launch (start us, length us, event | category | flops | bytes accessed | tf_op | source)
XLA Modules:
  0.0 68.0 jit_solution(6577422255579547806)
XLA Ops:
  0.6 65.1 %shard_map.84 = (bf16[8,1024]{1,0:T(8,128)(2,1)}, bf16[1024,256]{1,0:T(8,128)(2,1)}, bf16[1024,256]{1,0:T(8,128)(2,1)}, bf16[256,1024]{1,0:T(8,128)(2,1)}) custom-call(bf16[8,1024]{1,0:T(8,128)(2,1)} %act_ref.1, bf16[8,1024]{1,0:T(8,128)(2,1)} %grad_ref.1, bf16[1024,256]{1,0:T(8,128)(2,1)} %wg_hbm.1, bf16[1024,256]{1,0:T(8,128)(2,1)} %wu_hbm.1, ...), custom_call_target="tpu_custom_call" | custom-call | flops 2200000000 | bytes 3200000 | tf_op jit(solution)/shard_map/pallas_call | solution.py:305
  65.8 2.3 %shard_map.85 = (bf16[8,1024]{1,0:T(8,128)(2,1)}, bf16[1024,256]{1,0:T(8,128)(2,1)}, bf16[1024,256]{1,0:T(8,128)(2,1)}, bf16[256,1024]{1,0:T(8,128)(2,1)}) custom-call(bf16[8,1024]{1,0:T(8,128)(2,1)} %get-tuple-element.8.refs_0_, bf16[1024,256]{1,0:T(8,128)(2,1)} %get-tuple-element.9.refs_1_, bf16[1024,256]{1,0:T(8,128)(2,1)} %get-tuple-element.10.refs_2_, ...), custom_call_target="tpu_custom_call" | custom-call | tf_op jit(solution)/shard_map/pallas_call | solution.py:289

commit v4 on v3

--- a/solution.py
+++ b/solution.py
@@ -11,6 +11,8 @@
 CHUNKS = 8
 OWN = 15
 WA = 256
+FAR_ROWS = (4, 3, 5, 2, 6, 1, 7)
+FAR_Y = (2, 1, 3)
 NT = (((1,), (1,)), ((), ()))
 TN = (((0,), (0,)), ((), ()))
 
@@ -31,11 +33,11 @@
 
 
 def kernel(
-    act_ref, grad_ref, wg_hbm, wu_hbm, wd_hbm,
+    act_hbm, grad_hbm, wg_hbm, wu_hbm, wd_hbm,
     ig_hbm, gg_hbm, ug_hbm, dg_hbm,
-    xa, xb, acts, grads, wg, wu, wd, part, own_part, bsend, brecv, delta, deltas,
+    act_ref, grad_ref, xa, xb, acts, grads, wg, wu, wd, part, own_part, bsend, brecv, delta, deltas,
     total, own_total, ysend, yrecv, own_z, zsend, zrecv, ig, gg, ug, dg,
-    w_sem, o_sem, xa_recv, xb_recv, y0_recv, y_recv, b_recv, c_recv, dy_recv, dz_recv,
+    in_sem, w_sem, o_sem, xa_recv, xb_recv, y0_recv, y_recv, b_recv, c_recv, dy_recv, dz_recv,
     xa_send, xb_send, y0_send, y_send, b_send, c_send, dy_send, dz_send,
 ):
     r = lax.axis_index("rows")
@@ -63,6 +65,20 @@
     def drain(ref, sem):
         pltpu.make_async_copy(ref, ref, sem).wait()
 
+    in_copies = [
+        pltpu.make_async_copy(act_hbm, act_ref, in_sem.at[0]),
+        pltpu.make_async_copy(grad_hbm, grad_ref, in_sem.at[1]),
+    ]
+    for c in in_copies:
+        c.start()
+
+    barrier = pltpu.get_barrier_semaphore()
+    peers = [row_peer(k) for k in range(1, NR)]
+    peers += [y_peer(k) for k in range(1, NY)]
+    peers += [z_peer(k) for k in range(1, NZ)]
+    for p in peers:
+        pl.semaphore_signal(barrier, inc=1, device_id=p, device_id_type=pl.DeviceIdType.MESH)
+
     w_copies = [
         pltpu.make_async_copy(src, dst, w_sem.at[i])
         for i, (src, dst) in enumerate(((wg_hbm, wg), (wu_hbm, wu), (wd_hbm, wd)))
@@ -70,24 +86,20 @@
     for c in w_copies:
         c.start()
 
+    for c in in_copies:
+        c.wait()
+
     mine = jnp.concatenate([act_ref[...].astype(F32), grad_ref[...].astype(F32)], axis=0).astype(BF)
     xa[OWN, y] = mine[:, :WA]
     xb[OWN, y] = mine[:, WA:]
-
-    barrier = pltpu.get_barrier_semaphore()
-    peers = [row_peer(k) for k in range(1, NR)]
-    peers += [y_peer(k) for k in range(1, NY)]
-    peers += [z_peer(k) for k in range(1, NZ)]
-    for p in peers:
-        pl.semaphore_signal(barrier, inc=1, device_id=p, device_id_type=pl.DeviceIdType.MESH)
     pl.semaphore_wait(barrier, len(peers))
 
     def y_forward(slot):
-        for k in range(1, NY):
+        for k in FAR_Y:
             send(xb.at[slot, y], xb.at[slot, y], y_send.at[slot], y_recv.at[slot], y_peer(k))
 
     def start_gather():
-        for k in range(1, NY):
+        for k in FAR_Y:
             send(xa.at[OWN, y], xa.at[OWN, y], y0_send, y0_recv, y_peer(k))
         for to, k in ((2, 2), (3, -2), (0, 1), (1, -1)):
             send(xb.at[OWN, y], xb.at[to, y], xb_send.at[OWN], xb_recv.at[to], z_peer(k))
@@ -157,7 +169,7 @@
             v = part[8 * k:8 * k + 8, :]
             bsend[c, k] = jnp.concatenate([v[:, :384], v[:, 384:]], axis=0).astype(BF)
         own_part[c] = part[pl.ds(pl.multiple_of(r * 8, 8), 8)]
-        for k in range(1, NR):
+        for k in FAR_ROWS:
             send(bsend.at[c, lax.rem(r + k, NR)], brecv.at[c, k - 1], b_send.at[c], b_recv.at[c], row_peer(k))
 
     def pointwise(c):
@@ -175,7 +187,7 @@
         first = jnp.concatenate([hidden, gate_delta[:, :128]], axis=1)
         second = jnp.concatenate([gate_delta[:, 128:], up_delta], axis=1)
         delta[c, r] = jnp.concatenate([first, second], axis=0).astype(BF)
-        for k in range(1, NR):
+        for k in FAR_ROWS:
             send(delta.at[c, r], delta.at[c, r], c_send.at[c], c_recv.at[c], row_peer(k))
 
     def input_terms(c):
@@ -192,7 +204,7 @@
             ysend[c, k] = jnp.concatenate([total[0, k], total[1, k]], axis=0).astype(BF)
         for s in range(2):
             own_total[c, s] = total[s, y]
-        for k in range(1, NY):
+        for k in FAR_Y:
             send(ysend.at[c, lax.rem(y + k, NY)], yrecv.at[c, k - 1], dy_send.at[c], dy_recv.at[c], y_peer(k))
 
     def slot_offset(slot):
@@ -298,7 +310,6 @@
 
 
 def body(activations, out_grad, w_gate, w_up, w_down):
-    vmem = pl.BlockSpec(memory_space=pltpu.VMEM)
     hbm = pl.BlockSpec(memory_space=pltpu.HBM)
     any_space = pl.BlockSpec(memory_space=pl.ANY)
     dma = pltpu.SemaphoreType.DMA
@@ -310,9 +321,11 @@
             jax.ShapeDtypeStruct((1024, 256), BF),
             jax.ShapeDtypeStruct((256, 1024), BF),
         ),
-        in_specs=[vmem, vmem, hbm, hbm, hbm],
+        in_specs=[hbm] * 5,
         out_specs=(any_space, any_space, any_space, any_space),
         scratch_shapes=[
+            pltpu.VMEM((8, 1024), BF),
+            pltpu.VMEM((8, 1024), BF),
             pltpu.VMEM((16, 4, 16, WA), BF),
             pltpu.VMEM((16, 4, 16, 1024 - WA), BF),
             pltpu.VMEM((512, 1024), BF),
@@ -337,7 +350,7 @@
             pltpu.VMEM((1024, 256), BF),
             pltpu.VMEM((1024, 256), BF),
             pltpu.VMEM((256, 1024), BF),
-            dma((3,)), dma((4,)),
+            dma((2,)), dma((3,)), dma((4,)),
             dma((18,)), dma((16,)), dma, dma((16,)), dma((CHUNKS,)), dma((CHUNKS,)), dma((CHUNKS,)), dma,
             dma((18,)), dma((16,)), dma, dma((16,)), dma((CHUNKS,)), dma((CHUNKS,)), dma((CHUNKS,)), dma,
         ],

time: 69.2 us -> 68.1 us (0.984)
  no operation moved by 1% of the time
where the time goes in v4:
time: 68.1 us; the launch traced here: 67.6 us
  Pallas kernels  66.9 us (98%)
    pallas_call x1, Pallas kernels, body(): pl.pallas_call(kernel, out_shape=(jax.ShapeDtypeStruct((8, 1024), BF), ja...  64.7 us
    pallas_call x1, Pallas kernels, write_out(): pl.pallas_call(copy_kernel, out_shape=tuple((jax.ShapeDtypeStruct(a.shape...  2.27 us

profile of v4, /device:TPU:1, one launch (start us, length us, event | category | flops | bytes accessed | tf_op | source)
XLA Modules:
  0.0 67.6 jit_solution(14313619932448459157)
XLA Ops:
  0.6 64.7 %shard_map.84 = (bf16[8,1024]{1,0:T(8,128)(2,1)}, bf16[1024,256]{1,0:T(8,128)(2,1)}, bf16[1024,256]{1,0:T(8,128)(2,1)}, bf16[256,1024]{1,0:T(8,128)(2,1)}) custom-call(bf16[8,1024]{1,0:T(8,128)(2,1)} %act_hbm.1, bf16[8,1024]{1,0:T(8,128)(2,1)} %grad_hbm.1, bf16[1024,256]{1,0:T(8,128)(2,1)} %wg_hbm.1, bf16[1024,256]{1,0:T(8,128)(2,1)} %wu_hbm.1, ...), custom_call_target="tpu_custom_call" | custom-call | flops 2200000000 | bytes 3200000 | tf_op jit(solution)/shard_map/pallas_call | solution.py:316
  65.3 2.3 %shard_map.85 = (bf16[8,1024]{1,0:T(8,128)(2,1)}, bf16[1024,256]{1,0:T(8,128)(2,1)}, bf16[1024,256]{1,0:T(8,128)(2,1)}, bf16[256,1024]{1,0:T(8,128)(2,1)}) custom-call(bf16[8,1024]{1,0:T(8,128)(2,1)} %get-tuple-element.8.refs_0_, bf16[1024,256]{1,0:T(8,128)(2,1)} %get-tuple-element.9.refs_1_, bf16[1024,256]{1,0:T(8,128)(2,1)} %get-tuple-element.10.refs_2_, ...), custom_call_target="tpu_custom_call" | custom-call | tf_op jit(solution)/shard_map/pallas_call | solution.py:301

commit v5 on v4

--- a/solution.py
+++ b/solution.py
@@ -73,9 +73,10 @@
         c.start()
 
     barrier = pltpu.get_barrier_semaphore()
-    peers = [row_peer(k) for k in range(1, NR)]
-    peers += [y_peer(k) for k in range(1, NY)]
-    peers += [z_peer(k) for k in range(1, NZ)]
+    peers = [z_peer(k) for k in (8, 7, 9, 6, 10, 5, 11, 4, 12, 3, 13, 2, 14)]
+    peers += [row_peer(k) for k in FAR_ROWS]
+    peers += [y_peer(k) for k in FAR_Y]
+    peers += [z_peer(k) for k in (1, 15)]
     for p in peers:
         pl.semaphore_signal(barrier, inc=1, device_id=p, device_id_type=pl.DeviceIdType.MESH)
 

time: 68.1 us -> 67 us (0.984)
  Pallas kernels: 66.9 us -> 66.1 us
    pallas_call x1, Pallas kernels: 64.7 us -> 63.8 us  [body(): pl.pallas_call(kernel, out_shape=(jax.ShapeDtypeStruct((8, 1024), BF), ja...]
where the time goes in v5:
time: 67 us; the launch traced here: 66.7 us
  Pallas kernels  66.1 us (99%)
    pallas_call x1, Pallas kernels, body(): pl.pallas_call(kernel, out_shape=(jax.ShapeDtypeStruct((8, 1024), BF), ja...  63.8 us
    pallas_call x1, Pallas kernels, write_out(): pl.pallas_call(copy_kernel, out_shape=tuple((jax.ShapeDtypeStruct(a.shape...  2.27 us

profile of v5, /device:TPU:1, one launch (start us, length us, event | category | flops | bytes accessed | tf_op | source)
XLA Modules:
  0.0 66.7 jit_solution(15506467380178018209)
XLA Ops:
  0.6 63.8 %shard_map.84 = (bf16[8,1024]{1,0:T(8,128)(2,1)}, bf16[1024,256]{1,0:T(8,128)(2,1)}, bf16[1024,256]{1,0:T(8,128)(2,1)}, bf16[256,1024]{1,0:T(8,128)(2,1)}) custom-call(bf16[8,1024]{1,0:T(8,128)(2,1)} %act_hbm.1, bf16[8,1024]{1,0:T(8,128)(2,1)} %grad_hbm.1, bf16[1024,256]{1,0:T(8,128)(2,1)} %wg_hbm.1, bf16[1024,256]{1,0:T(8,128)(2,1)} %wu_hbm.1, ...), custom_call_target="tpu_custom_call" | custom-call | flops 2200000000 | bytes 3200000 | tf_op jit(solution)/shard_map/pallas_call | solution.py:317
  64.5 2.3 %shard_map.85 = (bf16[8,1024]{1,0:T(8,128)(2,1)}, bf16[1024,256]{1,0:T(8,128)(2,1)}, bf16[1024,256]{1,0:T(8,128)(2,1)}, bf16[256,1024]{1,0:T(8,128)(2,1)}) custom-call(bf16[8,1024]{1,0:T(8,128)(2,1)} %get-tuple-element.8.refs_0_, bf16[1024,256]{1,0:T(8,128)(2,1)} %get-tuple-element.9.refs_1_, bf16[1024,256]{1,0:T(8,128)(2,1)} %get-tuple-element.10.refs_2_, ...), custom_call_target="tpu_custom_call" | custom-call | tf_op jit(solution)/shard_map/pallas_call | solution.py:302
